TPU v7x, 32 devices: a whole 2x2x4 slice. The times are simulated.
32 devices in a mesh: dp: 2 (over core), ctx: 16 (over z, y, x).
Axes of the slice: x: 2, y: 2, z: 4, core: 2. Of those that a mesh axis runs over, the one named last changes fastest.
Arguments:
- pre_gate: bfloat16 [2, 2048, 2048], P('dp', 'ctx'), may hold values from -6 to 6
- post_gate: bfloat16 [2, 2048, 2048], P('dp', 'ctx'), may hold values from -6 to 6
- values: bfloat16 [2, 2048, 2048], P('dp', 'ctx'), may hold values from -6 to 6
- conv_out: bfloat16 [2, 2048, 2048], P('dp', 'ctx'), may hold values from -6 to 6
- grad_out: bfloat16 [2, 2048, 2048], P('dp', 'ctx'), may hold values from -6 to 6
- filter_param: bfloat16 [2048, 2048], P('ctx'), may hold values from -6 to 6
Outputs:
- d_pre_gate: bfloat16 [2, 2048, 2048], P('dp', 'ctx')
- d_post_gate: bfloat16 [2, 2048, 2048], P('dp', 'ctx')
- d_values: bfloat16 [2, 2048, 2048], P('dp', 'ctx')
- d_filter: float32 [2048, 2048], P(('ctx', 'dp'))
All inputs are finite; a program needn't handle non-finite values.
Results may differ from a plain program's by a relative error of at most 0.0058.
Values may be sent and summed in bfloat16 or wider, within the bound.
A program may use at most 64 MiB of HBM per device.

v0:
```python
import functools
import math

import jax
import jax.numpy as jnp
import ml_dtypes
import numpy as np
from jax import lax
from jax.experimental import pallas as pl
from jax.experimental.pallas import tpu as pltpu
from jax.sharding import PartitionSpec as P

MESH = pl.DeviceIdType.MESH


def add(a, b):
    return b if a is None else a if b is None else a + b


def sub(a, b):
    return a if b is None else -b if a is None else a - b


def scale(a, c):
    return None if a is None or c == 0.0 else a if c == 1.0 else -a if c == -1.0 else a * c


def turn(x, k, n):
    re, im = x
    c, s = math.cos(2 * math.pi * k / n), -math.sin(2 * math.pi * k / n)
    c, s = (0.0 if abs(v) < 1e-9 else round(v) if abs(abs(v) - 1) < 1e-9 else v for v in (c, s))
    c, s = float(c), float(s)
    if c and abs(abs(c) - abs(s)) < 1e-9 and re is not None and im is not None:
        if c * s > 0:
            return scale(re - im, c), scale(re + im, c)
        return scale(re + im, c), scale(im - re, c)
    return sub(scale(re, c), scale(im, s)), add(scale(im, c), scale(re, s))


def real_dft(xs):
    n = len(xs)
    if n == 1:
        return [(xs[0], None)]
    if n == 2:
        return [(add(xs[0], xs[1]), None), (sub(xs[0], xs[1]), None)]
    even, odd = real_dft(xs[0::2]), real_dft(xs[1::2])
    out = [None] * (n // 2 + 1)
    for k in range(n // 4 + 1):
        o = turn(odd[k], k, n)
        e = even[k]
        out[n // 2 - k] = (sub(e[0], o[0]), sub(o[1], e[1]))
        out[k] = (add(e[0], o[0]), add(e[1], o[1]))
    return out


def real_inverse(bins, n):
    if n == 2:
        return [bins[0][0] + bins[1][0]]
    even, odd = [], []
    for k in range(n // 4 + 1):
        a, b = bins[k], bins[n // 2 - k]
        even.append((add(a[0], b[0]), sub(a[1], b[1])))
        odd.append(turn((sub(a[0], b[0]), add(a[1], b[1])), -k, n))
    half = n // 2
    for part in (even, odd):
        part[0] = (part[0][0], None)
        part[-1] = (part[-1][0], None)
    first, second = real_inverse(even, half), real_inverse(odd, half)
    out = []
    for a, b in zip(first, second):
        out += [a, b]
    return out


def dft_tables(blocks, size):
    groups, whole = blocks + 1, 2 * blocks * size
    g = np.arange(groups)[:, None, None]
    h = np.arange(size)[None, :, None]
    s = np.arange(size)[None, None, :]
    angle = 2 * np.pi / whole * ((s * (2 * blocks * h + g)) % whole)
    c, n = np.cos(angle), np.sin(angle)
    forward = np.concatenate([np.concatenate([c, n], 2), np.concatenate([-n, c], 2)], 1)
    inverse = np.swapaxes(forward, 1, 2) / whole
    return forward.astype(ml_dtypes.bfloat16), inverse.astype(ml_dtypes.bfloat16)


def kernel(
    blocks, size, factor_k, factor_d,
    pre_h, post_h, val_h, grad_h, fil_h, fwd_h, inv_h,
    back_ref, dfil_ref,
    pre, post, val, grad, fil, fwd, inv,
    send, recv, taps, spectra, kspec, gspec, turned, dterm, dwide, dgot,
    load_sem, send_sem, recv_sem, dsem,
):
    me = lax.axis_index("ctx")
    core = lax.axis_index("dp")
    groups = blocks + 1
    f32, bf16 = jnp.float32, jnp.bfloat16
    half = size // 2

    loads = []
    for i, (a, b) in enumerate(
        [(grad_h, grad), (post_h, post), (pre_h, pre), (val_h, val), (fil_h, fil),
         (fwd_h, fwd), (inv_h, inv)]
    ):
        loads.append(pltpu.make_async_copy(a, b, load_sem.at[i]))
        if i < 2:
            loads[-1].start()

    barrier = pltpu.get_barrier_semaphore()

    @pl.loop(1, blocks)
    def _(k):
        pl.semaphore_signal(
            barrier, inc=1, device_id=(core, lax.rem(me + k, blocks)), device_id_type=MESH
        )

    pl.semaphore_signal(barrier, inc=1, device_id=(1 - core, me), device_id_type=MESH)

    def copy(phase, other, slot):
        return pltpu.make_async_remote_copy(
            src_ref=send.at[phase, other],
            dst_ref=recv.at[phase, slot],
            send_sem=send_sem.at[phase, other],
            recv_sem=recv_sem.at[phase, slot],
            device_id=(core, other),
            device_id_type=MESH,
        )

    def product(phase, a, b, j):
        cols = pl.ds(pl.multiple_of(j * size, size), size)
        send[phase, j] = (a[:, cols].astype(f32) * b[:, cols].astype(f32)).astype(bf16)

    def product_and_start(phase, a, b):
        @pl.loop(1, blocks)
        def _(k):
            other = lax.rem(me + k, blocks)
            product(phase, a, b, other)
            copy(phase, other, me).start()

        product(phase, a, b, me)
        recv[phase, me] = send[phase, me]

    def start_all(phase):
        @pl.loop(1, blocks)
        def _(k):
            copy(phase, lax.rem(me + k, blocks), me).start()

        recv[phase, me] = send[phase, me]

    def wait_recv_all(phase):
        @pl.loop(1, blocks)
        def _(k):
            other = lax.rem(me + k, blocks)
            copy(phase, other, other).wait_recv()

    def wait_send_all(phase):
        @pl.loop(1, blocks)
        def _(k):
            copy(phase, lax.rem(me + k, blocks), me).wait_send()

    def split(read):
        @pl.loop(0, size // 16)
        def _(i):
            rows = pl.ds(pl.multiple_of(i * 16, 16), 16)
            lower = pl.ds(pl.multiple_of(i * 16 + size, 16), 16)
            xs = [read(q, rows).astype(f32) for q in range(blocks)] + [None] * blocks
            for g, (re, im) in enumerate(real_dft(xs)):
                spectra[g, rows, :] = re.astype(bf16)
                if im is None:
                    im = jnp.zeros_like(re)
                spectra[g, lower, :] = im.astype(bf16)

    def over_groups(body):
        @pl.loop(0, blocks // 4)
        def _(i):
            for u in range(4):
                body(i * 4 + u)

        body(blocks)

    def spectrum(g):
        return jnp.dot(fwd[g], spectra[g], preferred_element_type=f32)

    def back_to_time(g, re, im):
        both = jnp.concatenate([re.astype(bf16), im.astype(bf16)], axis=0)
        turned[g] = jnp.dot(inv[g], both, preferred_element_type=f32)

    def join(write):
        @pl.loop(0, size // 16)
        def _(i):
            rows = pl.ds(pl.multiple_of(i * 16, 16), 16)
            lower = pl.ds(pl.multiple_of(i * 16 + size, 16), 16)
            bins = []
            for g in range(groups):
                im = None if g in (0, blocks) else turned[g, lower, :]
                bins.append((turned[g, rows, :], im))
            for q, y in enumerate(real_inverse(bins, 2 * blocks)):
                write(q, rows, y)

    loads[0].wait()
    loads[1].wait()
    for load in loads[2:]:
        load.start()
    pl.semaphore_wait(barrier, blocks)
    product_and_start(0, grad, post)
    loads[2].wait()
    loads[3].wait()
    wait_send_all(0)
    product_and_start(1, pre, val)

    loads[4].wait()

    @pl.loop(0, blocks)
    def _(q):
        cols = pl.ds(pl.multiple_of(q * size, size), size)
        taps[q] = fil[:, cols].astype(f32).T.astype(bf16)

    split(lambda q, rows: taps[q, rows, :])
    loads[5].wait()

    def keep_kernel(g):
        kspec[g] = spectrum(g) * factor_k

    over_groups(keep_kernel)
    loads[6].wait()

    wait_recv_all(0)
    split(lambda q, rows: recv[0, q, rows, :])

    def back_group(g):
        x = spectrum(g)
        gspec[g] = x
        gr, gi = x[:size], x[size:]
        kr, ki = kspec[g, :size], kspec[g, size:]
        back_to_time(g, kr * gr + ki * gi, kr * gi - ki * gr)

    over_groups(back_group)

    def keep_back(q, rows, y):
        send[2, q, rows, :] = y.astype(bf16)

    join(keep_back)
    start_all(2)

    wait_recv_all(1)
    split(lambda q, rows: recv[1, q, rows, :])

    def filter_group(g):
        x = spectrum(g)
        mr, mi = x[:size], x[size:]
        gr, gi = gspec[g, :size], gspec[g, size:]
        back_to_time(g, (gr * mr + gi * mi) * factor_d, (gi * mr - gr * mi) * factor_d)

    over_groups(filter_group)

    def keep_term(q, rows, y):
        dterm[q, rows, :] = y

    join(keep_term)

    @pl.loop(0, blocks)
    def _(q):
        cols = pl.ds(pl.multiple_of(q * size, size), size)
        dwide[:, cols] = dterm[q].T

    theirs = pl.ds(pl.multiple_of((1 - core) * half, 8), half)
    ours = pl.ds(pl.multiple_of(core * half, 8), half)
    pair = pltpu.make_async_remote_copy(
        src_ref=dwide.at[theirs, :],
        dst_ref=dgot,
        send_sem=dsem.at[0],
        recv_sem=dsem.at[1],
        device_id=(1 - core, me),
        device_id_type=MESH,
    )
    pair.start()

    wait_recv_all(2)

    @pl.loop(0, blocks)
    def _(j):
        cols = pl.ds(pl.multiple_of(j * size, size), size)
        back_ref[:, cols] = recv[2, j]

    pair.wait_recv()
    dfil_ref[...] = dwide[ours, :] + dgot[...]

    pair.wait_send()
    wait_send_all(1)
    wait_send_all(2)


def write_out(back, pre, val, grad, conv, d_fil, d_pre, d_post, d_val, d_out):
    f32, bf16 = jnp.float32, jnp.bfloat16
    b = back[...].astype(f32)
    d_pre[...] = (b * val[...].astype(f32)).astype(bf16)
    d_val[...] = (b * pre[...].astype(f32)).astype(bf16)
    d_post[...] = (grad[...].astype(f32) * conv[...].astype(f32)).astype(bf16)
    d_out[...] = d_fil[...]


def fast(pre_gate, post_gate, values, conv_out, grad_out, filter_param):
    blocks = lax.axis_size("ctx")
    size, channels = pre_gate.shape[1:]
    length = filter_param.shape[1]
    fwd, inv = dft_tables(blocks, size)
    rows = (size, channels)
    f32, bf16 = jnp.float32, jnp.bfloat16
    grid_block = (blocks, size, size)
    spec_block = (blocks + 1, 2 * size, size)
    vmem = pl.BlockSpec(memory_space=pltpu.VMEM)
    body = functools.partial(
        kernel, blocks, size, length ** (-0.5), 1.0 / (lax.axis_size("dp") * math.sqrt(length))
    )
    results = pl.pallas_call(
        body,
        out_shape=[
            jax.ShapeDtypeStruct(rows, bf16),
            jax.ShapeDtypeStruct((size // 2, length), f32),
        ],
        in_specs=[pl.BlockSpec(memory_space=pltpu.HBM)] * 7,
        out_specs=[vmem] * 2,
        scratch_shapes=[pltpu.VMEM(rows, bf16)] * 4
        + [
            pltpu.VMEM((size, length), bf16),
            pltpu.VMEM(fwd.shape, bf16),
            pltpu.VMEM(inv.shape, bf16),
            pltpu.VMEM((3,) + grid_block, bf16),
            pltpu.VMEM((3,) + grid_block, bf16),
            pltpu.VMEM(grid_block, bf16),
            pltpu.VMEM(spec_block, bf16),
            pltpu.VMEM(spec_block, f32),
            pltpu.VMEM(spec_block, f32),
            pltpu.VMEM(spec_block, f32),
            pltpu.VMEM(grid_block, f32),
            pltpu.VMEM((size, length), f32),
            pltpu.VMEM((size // 2, length), f32),
            pltpu.SemaphoreType.DMA((7,)),
            pltpu.SemaphoreType.DMA((3, blocks)),
            pltpu.SemaphoreType.DMA((3, blocks)),
            pltpu.SemaphoreType.DMA((2,)),
        ],
        compiler_params=pltpu.CompilerParams(
            collective_id=0, has_side_effects=True, vmem_limit_bytes=62 * 2**20
        ),
        name="hyena_backward",
    )(pre_gate[0], post_gate[0], values[0], grad_out[0], filter_param,
      jnp.asarray(fwd), jnp.asarray(inv))
    steps = 2
    block = pl.BlockSpec((size // steps, channels), lambda i: (i, 0))
    part = pl.BlockSpec((size // 2 // steps, length), lambda i: (i, 0))
    d_pre, d_post, d_val, d_fil = pl.pallas_call(
        write_out,
        grid=(steps,),
        out_shape=[jax.ShapeDtypeStruct(rows, bf16)] * 3
        + [jax.ShapeDtypeStruct((size // 2, length), f32)],
        in_specs=[block] * 5 + [part],
        out_specs=[block] * 3 + [part],
        name="write_out",
    )(results[0], pre_gate[0], values[0], grad_out[0], conv_out[0], results[1])
    return d_pre[None], d_post[None], d_val[None], d_fil


SECTION = 128


exact = lax.Precision.HIGHEST
full_turn = 2.0 * math.pi


def general_tables(section, inner, whole):
    rows = jnp.arange(section, dtype=jnp.int32)
    half_rows = jnp.arange(section // 2, dtype=jnp.int32)
    columns = jnp.arange(inner, dtype=jnp.int32)
    first = (
        -full_turn / section * (rows[:, None] * half_rows[None, :] % section).astype(jnp.float32)
    )
    twist = -full_turn / whole * (rows[:, None] * columns[None, :] % whole).astype(jnp.float32)
    second = -full_turn / inner * (columns[:, None] * columns[None, :] % inner).astype(jnp.float32)
    first_cos = jnp.cos(first)
    first_sin = jnp.sin(first)
    second_cos = jnp.cos(second)
    second_sin = jnp.sin(second)
    single_table = jnp.concatenate([first_cos, first_sin], axis=0)
    paired_table = jnp.concatenate(
        [
            jnp.concatenate([first_cos, -first_sin], axis=1),
            jnp.concatenate([first_sin, first_cos], axis=1),
        ],
        axis=0,
    )
    later_forward = jnp.concatenate(
        [
            jnp.concatenate([second_cos, second_sin], axis=1),
            jnp.concatenate([-second_sin, second_cos], axis=1),
        ],
        axis=0,
    )
    later_inverse = jnp.concatenate(
        [
            jnp.concatenate([second_cos, -second_sin], axis=1),
            jnp.concatenate([second_sin, second_cos], axis=1),
        ],
        axis=0,
    )
    return (
        single_table,
        paired_table,
        jnp.cos(twist),
        jnp.sin(twist),
        later_forward,
        later_inverse,
    )


def forward(signal, tables, paired):
    single_table, paired_table, twist_cos, twist_sin, later_forward, later_inverse = tables
    table = paired_table if paired else single_table
    section_one = jnp.einsum("ja,cab->cjb", table, signal, precision=exact)
    count = twist_cos.shape[0]
    real_one = section_one[:, :count]
    imag_one = section_one[:, count:]
    joined = jnp.concatenate(
        [real_one * twist_cos - imag_one * twist_sin, real_one * twist_sin + imag_one * twist_cos],
        axis=2,
    )
    return jnp.einsum("ckb,bm->ckm", joined, later_forward, precision=exact)


def inverse(spectrum, tables):
    single_table, paired_table, twist_cos, twist_sin, later_forward, later_inverse = tables
    inner = twist_cos.shape[1]
    section_two = jnp.einsum("ckm,mb->ckb", spectrum, later_inverse, precision=exact)
    real_two = section_two[..., :inner]
    imag_two = section_two[..., inner:]
    stacked = jnp.concatenate(
        [real_two * twist_cos + imag_two * twist_sin, imag_two * twist_cos - real_two * twist_sin],
        axis=1,
    )
    scale = 1.0 / (twist_cos.shape[0] * inner)
    signal = jnp.einsum("ja,cjb->cab", paired_table, stacked, precision=exact) * scale
    channels = signal.shape[0]
    middle = signal.shape[1] // 2
    return (signal[:, :middle].reshape(channels, -1), signal[:, middle:].reshape(channels, -1))


def mirror(part):
    flipped = part[:, ::-1, ::-1]
    shifted = jnp.roll(flipped, 1, axis=1)
    zero_row = jnp.roll(part[:, 0, ::-1], 1, axis=1)
    return jnp.concatenate([zero_row[:, None], shifted[:, 1:]], axis=1)


def general(pre_gate, post_gate, values, conv_out, grad_out, filter_param):
    gate_rows = pre_gate[0].astype(jnp.float32)
    post_rows = post_gate[0].astype(jnp.float32)
    value_rows = values[0].astype(jnp.float32)
    grad_rows = grad_out[0].astype(jnp.float32)
    mixed = (gate_rows * value_rows).astype(jnp.bfloat16)
    grad_conv = (grad_rows * post_rows).astype(jnp.bfloat16)
    d_post = (grad_rows * conv_out[0].astype(jnp.float32)).astype(jnp.bfloat16)
    length = filter_param.shape[1]
    whole = 2 * length
    inner = whole // SECTION
    half_section = SECTION // 2
    tables = general_tables(SECTION, inner, whole)
    kernel = (filter_param.astype(jnp.float32) * length ** (-0.5)).reshape(-1, half_section, inner)
    mixed_cols = mixed.T
    grad_cols = grad_conv.T
    mixed_chan, grad_chan = (
        lax.all_to_all(mixed_cols, "ctx", split_axis=0, concat_axis=1, tiled=True),
        lax.all_to_all(grad_cols, "ctx", split_axis=0, concat_axis=1, tiled=True),
    )
    kernel_spec = forward(kernel, tables, False)
    channels = mixed_chan.shape[0]
    both_signals = jnp.concatenate(
        [
            mixed_chan.reshape(channels, half_section, inner),
            grad_chan.reshape(channels, half_section, inner),
        ],
        axis=1,
    ).astype(jnp.float32)
    packed = forward(both_signals, tables, True)
    packed_real = packed[..., :inner]
    packed_imag = packed[..., inner:]
    mirror_real = mirror(packed_real)
    mirror_imag = mirror(packed_imag)
    mixed_real = 0.5 * (packed_real + mirror_real)
    mixed_imag = 0.5 * (packed_imag - mirror_imag)
    grad_real = 0.5 * (packed_imag + mirror_imag)
    grad_imag = 0.5 * (mirror_real - packed_real)
    kernel_real = kernel_spec[..., :inner]
    kernel_imag = kernel_spec[..., inner:]
    back_real = kernel_real * grad_real + kernel_imag * grad_imag
    back_imag = kernel_real * grad_imag - kernel_imag * grad_real
    factor = 1.0 / (lax.axis_size("dp") * math.sqrt(length))
    cross_real = (grad_real * mixed_real + grad_imag * mixed_imag) * factor
    cross_imag = (grad_imag * mixed_real - grad_real * mixed_imag) * factor
    joined = jnp.concatenate([back_real - cross_imag, back_imag + cross_real], axis=2)
    back_signal, terms = inverse(joined, tables)
    d_filter = lax.psum_scatter(terms, "dp", scatter_dimension=0, tiled=True)
    back_chan = back_signal.astype(jnp.bfloat16)
    back_rows = lax.all_to_all(back_chan, "ctx", split_axis=1, concat_axis=0, tiled=True).T.astype(
        jnp.float32
    )
    d_pre = (back_rows * value_rows).astype(jnp.bfloat16)
    d_val = (back_rows * gate_rows).astype(jnp.bfloat16)
    return (d_pre[None], d_post[None], d_val[None], d_filter)


def local(pre_gate, post_gate, values, conv_out, grad_out, filter_param):
    blocks = lax.axis_size("ctx")
    batch, size, channels = pre_gate.shape
    fits = (
        lax.axis_size("dp") == 2
        and batch == 1
        and size == 128
        and channels == 128 * blocks
        and filter_param.shape == (128, 128 * blocks)
        and blocks == 16
    )
    run = fast if fits else general
    return run(pre_gate, post_gate, values, conv_out, grad_out, filter_param)


def solution(mesh):
    return jax.shard_map(
        local,
        mesh=mesh,
        in_specs=(
            P("dp", "ctx", None),
            P("dp", "ctx", None),
            P("dp", "ctx", None),
            P("dp", "ctx", None),
            P("dp", "ctx", None),
            P("ctx", None),
        ),
        out_specs=(
            P("dp", "ctx", None),
            P("dp", "ctx", None),
            P("dp", "ctx", None),
            P(("ctx", "dp"), None),
        ),
        check_vma=False,
    )
```

profile of v0, /device:TPU:31, one launch (start us, length us, event | category | flops | bytes accessed | tf_op | source)
XLA Modules:
  0.0 47.9 jit_solution(7775786153984610049)
XLA Ops:
  0.6 44.4 %hyena_backward.1 = (bf16[128,2048]{1,0:T(8,128)(2,1)}, f32[64,2048]{1,0:T(8,128)}) custom-call(bf16[128,2048]{1,0:T(8,128)(2,1)} %bitcast.8, bf16[128,2048]{1,0:T(8,128)(2,1)} %bitcast.14, bf16[128,2048]{1,0:T(8,128)(2,1)} %bitcast.10, bf16[128,2048]{1,0:T(8,128)(2,1)} %bitcast.12, bf16[128,2048]{1,0:T(8,128)(2,1)} %fil_h.1, ...), custom_call_target="tpu_custom_call" | custom-call | tf_op jit(solution)/shard_map/hyena_backward/pallas_call | solution.py:316
  45.0 2.9 %write_out.1 = (bf16[128,2048]{1,0:T(8,128)(2,1)}, bf16[128,2048]{1,0:T(8,128)(2,1)}, bf16[128,2048]{1,0:T(8,128)(2,1)}, f32[64,2048]{1,0:T(8,128)}) custom-call(bf16[128,2048]{1,0:T(8,128)(2,1)} %get-tuple-element.10.back, bf16[128,2048]{1,0:T(8,128)(2,1)} %bitcast.9, bf16[128,2048]{1,0:T(8,128)(2,1)} %bitcast.11, bf16[128,2048]{1,0:T(8,128)(2,1)} %bitcast.13, ...), custom_call_target="tpu_custom_call" | custom-call | tf_op jit(solution)/shard_map/write_out/pallas_call | solution.py:353
where the time goes:
time: 48.1 us; the launch traced here: 47.9 us
  Pallas kernels  47.3 us (98%)
  between operations  0.64 us (1%)
    pallas_call x1, Pallas kernels, fast(): pl.pallas_call(body, out_shape=[jax.ShapeDtypeStruct(rows, bf16), jax.Sha...  44.4 us
    pallas_call x1, Pallas kernels, fast(): pl.pallas_call(write_out, grid=(steps,), out_shape=[jax.ShapeDtypeStruct(...  2.9 us

commit v1 on v0

--- a/solution.py
+++ b/solution.py
@@ -172,10 +172,10 @@
                 spectra[g, lower, :] = im.astype(bf16)
 
     def over_groups(body):
-        @pl.loop(0, blocks // 4)
+        @pl.loop(0, blocks // 8)
         def _(i):
-            for u in range(4):
-                body(i * 4 + u)
+            for u in range(8):
+                body(i * 8 + u)
 
         body(blocks)
 

time: 48.1 us -> 47.4 us (0.985)
  Pallas kernels: 47.3 us -> 46.6 us
    pallas_call x1, Pallas kernels: 44.4 us -> 43.7 us  [fast(): pl.pallas_call(body, out_shape=[jax.ShapeDtypeStruct(rows, bf16), jax.Sha...]
where the time goes in v1:
time: 47.4 us; the launch traced here: 47.3 us
  Pallas kernels  46.6 us (98%)
  between operations  0.64 us (1%)
    pallas_call x1, Pallas kernels, fast(): pl.pallas_call(body, out_shape=[jax.ShapeDtypeStruct(rows, bf16), jax.Sha...  43.7 us
    pallas_call x1, Pallas kernels, fast(): pl.pallas_call(write_out, grid=(steps,), out_shape=[jax.ShapeDtypeStruct(...  2.9 us

profile of v1, /device:TPU:31, one launch (start us, length us, event | category | flops | bytes accessed | tf_op | source)
XLA Modules:
  0.0 47.3 jit_solution(2019954850746414861)
XLA Ops:
  0.6 43.7 %hyena_backward.1 = (bf16[128,2048]{1,0:T(8,128)(2,1)}, f32[64,2048]{1,0:T(8,128)}) custom-call(bf16[128,2048]{1,0:T(8,128)(2,1)} %bitcast.8, bf16[128,2048]{1,0:T(8,128)(2,1)} %bitcast.14, bf16[128,2048]{1,0:T(8,128)(2,1)} %bitcast.10, bf16[128,2048]{1,0:T(8,128)(2,1)} %bitcast.12, bf16[128,2048]{1,0:T(8,128)(2,1)} %fil_h.1, ...), custom_call_target="tpu_custom_call" | custom-call | tf_op jit(solution)/shard_map/hyena_backward/pallas_call | solution.py:316
  44.4 2.9 %write_out.1 = (bf16[128,2048]{1,0:T(8,128)(2,1)}, bf16[128,2048]{1,0:T(8,128)(2,1)}, bf16[128,2048]{1,0:T(8,128)(2,1)}, f32[64,2048]{1,0:T(8,128)}) custom-call(bf16[128,2048]{1,0:T(8,128)(2,1)} %get-tuple-element.10.back, bf16[128,2048]{1,0:T(8,128)(2,1)} %bitcast.9, bf16[128,2048]{1,0:T(8,128)(2,1)} %bitcast.11, bf16[128,2048]{1,0:T(8,128)(2,1)} %bitcast.13, ...), custom_call_target="tpu_custom_call" | custom-call | tf_op jit(solution)/shard_map/write_out/pallas_call | solution.py:353
